TPU v7x, 32 devices: a whole 2x2x4 slice. The times are simulated.
32 devices in a mesh: row: 8 (over z, y), col: 4 (over x, core).
Axes of the slice: x: 2, y: 2, z: 4, core: 2. Of those that a mesh axis runs over, the one named last changes fastest.
Arguments:
- hidden: bfloat16 [128, 28672], P('col', 'row'), may hold values from -6 to 6
- down_weight: bfloat16 [28672, 8192], P('row', 'col'), may hold values from -0.03125 to 0.03125
- out_grad: bfloat16 [128, 8192], P('row', 'col'), may hold values from -6 to 6
Outputs:
- projected: bfloat16 [128, 8192], P('row', 'col')
- hidden_grad: bfloat16 [128, 28672], P('col', 'row')
- weight_grad: float32 [28672, 8192], P('row', 'col')
All inputs are finite; a program needn't handle non-finite values.
Results may differ from a plain program's by a relative error of at most 0.001.
Values may be sent and summed in bfloat16 or wider, within the bound.
A program may use at most 128 MiB of HBM per device.

v0:
```python
import jax
import jax.numpy as jnp
from jax import lax
from jax.sharding import PartitionSpec as P


def on_device(hidden, down_weight, out_grad):
    all_hidden = lax.all_gather(hidden, "col", axis=0, tiled=True)
    all_grad = lax.all_gather(out_grad, "row", axis=0, tiled=True)
    projected = lax.psum_scatter(
        jnp.dot(all_hidden, down_weight, preferred_element_type=jnp.float32),
        "row",
        scatter_dimension=0,
        tiled=True,
    ).astype(jnp.bfloat16)
    partial_grad = lax.dot_general(
        all_grad, down_weight, (((1,), (1,)), ((), ())), preferred_element_type=jnp.float32
    )
    hidden_grad = lax.psum_scatter(partial_grad, "col", scatter_dimension=0, tiled=True).astype(
        jnp.bfloat16
    )
    weight_grad = lax.dot_general(
        all_hidden, all_grad, (((0,), (0,)), ((), ())), preferred_element_type=jnp.float32
    )
    weight_grad = weight_grad / jnp.sqrt(jnp.float32(all_grad.shape[0]))
    return (projected, hidden_grad, weight_grad)


def solution(mesh):
    return jax.shard_map(
        on_device,
        mesh=mesh,
        in_specs=(P("col", "row"), P("row", "col"), P("row", "col")),
        out_specs=(P("row", "col"), P("col", "row"), P("row", "col")),
        check_vma=False,
    )
```

profile of v0, /device:TPU:0, one launch (start us, length us, event | category | flops | bytes accessed | tf_op | source)
XLA Modules:
  0.0 131.3 jit_solution(16371479501317082622)
XLA Ops:
  7.2 0.0 copy-start
  7.2 0.0 reduce-scatter.3.cloned.1.call-start
  7.2 11.0 %all_gather.6 = bf16[128,3584]{1,0:T(8,128)(2,1)S(1)} all-gather(bf16[32,3584]{1,0:T(8,128)(2,1)} %param.3), channel_id=1, replica_groups=mesh['row'=8,'col'=4] {'col'}, dimensions={0}, use_global_device_ids=true | all-gather | bytes 1146880 | tf_op jit(solution)/shard_map/all_gather | solution.py:8
  18.2 8.2 %fusion = f32[128,2048]{1,0:T(8,128)} fusion(bf16[128,3584]{1,0:T(8,128)(2,1)S(1)} %all_gather.6, bf16[3584,2048]{1,0:T(8,128)(2,1)} %param.4), kind=kOutput, calls=%fused_computation.1 | convolution fusion | flops 1879048192 | bytes 16646144 | tf_op jit(solution)/shard_map/dot_general | solution.py:11
  26.4 0.0 reduce-scatter.3.cloned.1.call-update
  26.5 0.0 reduce-scatter.5.cloned.1.call-start
  26.5 0.0 copy-done
  26.5 32.2 %all_gather.7 = bf16[128,2048]{1,0:T(8,128)(2,1)S(1)} all-gather(bf16[16,2048]{1,0:T(8,128)(2,1)S(1)} %copy-done), channel_id=1, replica_groups=mesh['row'=8,'col'=4] {'row'}, dimensions={0}, use_global_device_ids=true | all-gather | bytes 589824 | tf_op jit(solution)/shard_map/all_gather | solution.py:9
  58.7 11.4 %fusion.1 = f32[128,3584]{1,0:T(8,128)} fusion(bf16[128,2048]{1,0:T(8,128)(2,1)S(1)} %all_gather.7, bf16[3584,2048]{1,0:T(8,128)(2,1)} %param.4), kind=kOutput, calls=%fused_computation.2 | convolution fusion | flops 1879048192 | bytes 17039360 | tf_op jit(solution)/shard_map/dot_general | solution.py:16
  70.1 0.0 reduce-scatter.5.cloned.1.call-update
  70.1 12.4 %convolution_multiply_fusion = f32[3584,2048]{1,0:T(8,128)} fusion(bf16[128,3584]{1,0:T(8,128)(2,1)S(1)} %all_gather.6, bf16[128,2048]{1,0:T(8,128)(2,1)S(1)} %all_gather.7), kind=kOutput, calls=%fused_computation | convolution fusion | flops 1886388224 | bytes 30801920 | tf_op jit(solution)/shard_map/dot_general | solution.py:22
  82.6 8.6 %reduce-scatter.3.cloned.1.call-done = f32[16,2048]{1,0:T(8,128)} async-done(((f32[128,2048]{1,0:T(8,128)}), f32[16,2048]{1,0:T(8,128)}) %reduce-scatter.3.cloned.1.call-update) | async-done | bytes 131088 | tf_op jit(solution)/shard_map/reduce_scatter | solution.py:10
  91.2 1.5 %convert_element_type.6 = bf16[16,2048]{1,0:T(8,128)(2,1)} convert(f32[16,2048]{1,0:T(8,128)} %reduce-scatter.3.cloned.1.call-done) | non-fusion elementwise | flops 32768 | bytes 196608 | tf_op jit(solution)/shard_map/convert_element_type | solution.py:15
  92.7 30.0 %reduce-scatter.5.cloned.1.call-done = f32[32,3584]{1,0:T(8,128)} async-done(((f32[128,3584]{1,0:T(8,128)}), f32[32,3584]{1,0:T(8,128)}) %reduce-scatter.5.cloned.1.call-update) | async-done | bytes 458768 | tf_op jit(solution)/shard_map/reduce_scatter | solution.py:19
  122.7 1.7 %convert_element_type.7 = bf16[32,3584]{1,0:T(8,128)(2,1)} convert(f32[32,3584]{1,0:T(8,128)} %reduce-scatter.5.cloned.1.call-done) | non-fusion elementwise | flops 114688 | bytes 688128 | tf_op jit(solution)/shard_map/convert_element_type | solution.py:19
Async XLA Ops:
  7.2 19.3 %copy-start = (bf16[16,2048]{1,0:T(8,128)(2,1)S(1)}, bf16[16,2048]{1,0:T(8,128)(2,1)}, u32[]{:S(2)}) copy-start(bf16[16,2048]{1,0:T(8,128)(2,1)} %param.5) | copy-start | bytes 196612
  7.2 84.0 %reduce-scatter.3.cloned.1.call-start = ((), (), s32[]{:S(2)}) async-start(), calls=%async_computation.2 | async-start | bytes 1179648 | tf_op jit(solution)/shard_map/reduce_scatter | solution.py:10
  26.5 96.3 %reduce-scatter.5.cloned.1.call-start = ((), (), s32[]{:S(2)}) async-start(), calls=%async_computation.3 | async-start | bytes 2293760 | tf_op jit(solution)/shard_map/reduce_scatter | solution.py:19
Sparse Core Ops, SparseCore 0:
  26.6 64.5 reduce-scatter.2
  93.9 28.8 reduce-scatter.4
where the time goes:
time: 132 us; the launch traced here: 131 us
  blocking collectives  43.2 us (33%)
  waiting for transfers between devices  38.7 us (29%)
  matrix products  32 us (24%)
  between operations  14.1 us (11%)
  other arithmetic  3.27 us (2%)
    all_gather x1, blocking collectives, on_device(): all_grad = lax.all_gather(out_grad, 'row', axis=0, tiled=True)  32.2 us
    reduce_scatter x1, waiting for transfers between devices, on_device(): lax.psum_scatter(partial_grad, 'col', scatter_dimension=0, tiled=True)  30 us
    dot_general x1, matrix products, on_device(): lax.dot_general(all_hidden, all_grad, (((0,), (0,)), ((), ())), preferred...  12.4 us
    dot_general x1, matrix products, on_device(): lax.dot_general(all_grad, down_weight, (((1,), (1,)), ((), ())), preferre...  11.4 us
    all_gather x1, blocking collectives, on_device(): all_hidden = lax.all_gather(hidden, 'col', axis=0, tiled=True)  11 us
    reduce_scatter x1, waiting for transfers between devices, on_device(): lax.psum_scatter(jnp.dot(all_hidden, down_weight, preferred_element_type=...  8.62 us
    dot_general x1, matrix products, on_device(): jnp.dot(all_hidden, down_weight, preferred_element_type=jnp.float32)  8.24 us
  transfers between devices with their start and end apart: 2, of which 2 were waited for; matrix products, arithmetic and copies ran while one was open for 19% of the time, Pallas kernels for 0%

commit v1 on v0

v1 whole, which is shorter than its diff:
```python
import functools

import jax
import jax.numpy as jnp
from jax import lax
from jax.experimental import pallas as pl
from jax.experimental.pallas import tpu as pltpu
from jax.sharding import PartitionSpec as P

MESH = pl.DeviceIdType.MESH


def tile_of(extent, most):
    best = 128
    for width in range(128, most + 1, 128):
        if extent % width == 0:
            best = width
    return best


def exchange_kernel(
    nrow,
    ncol,
    hidden,
    weight,
    grad,
    proj_out,
    hgrad_out,
    all_hidden_out,
    all_grad_out,
    w,
    ah,
    ag,
    p_part,
    p_recv,
    p_recv_z,
    h_part,
    h_recv,
    h_recv_x,
    w_sem,
    own_sem,
    out_sem,
    hx_send,
    hx_recv,
    hc_send,
    hc_recv,
    gz_send,
    gz_recv,
    gy_send,
    gy_recv,
    py_send,
    py_recv,
    pz_send,
    pz_recv,
    qc_send,
    qc_recv,
    qx_send,
    qx_recv,
):
    nz, nx = nrow // 2, ncol // 2
    row, col = lax.axis_index("row"), lax.axis_index("col")
    z, y = row // 2, lax.rem(row, 2)
    x, core = col // 2, lax.rem(col, 2)
    sibling = (row, x * 2 + 1 - core)
    across = (z * 2 + 1 - y, col)

    def x_peer(d):
        return (row, lax.rem(x + d, nx) * 2 + core)

    def z_peer(d):
        return (lax.rem(z + d, nz) * 2 + y, col)

    def remote(src, dst, send, recv, device):
        return pltpu.make_async_remote_copy(
            src_ref=src, dst_ref=dst, send_sem=send, recv_sem=recv, device_id=device, device_id_type=MESH
        )

    hb, ff = hidden.shape
    gb, dd = grad.shape
    pieces = hx_recv.shape[0]
    wide = ff // pieces
    np_, tp = p_part.shape[0], p_part.shape[-1]
    nh, th = h_part.shape[0], h_part.shape[-1]

    w_copies = []
    for t in range(nh):
        rows = pl.ds(t * th, th)
        c = pltpu.make_async_copy(weight.at[rows], w.at[rows], w_sem.at[t])
        c.start()
        w_copies.append(c)

    def h_block(owner):
        return pl.ds(pl.multiple_of(owner * hb, hb), hb)

    def g_block(owner):
        return pl.ds(pl.multiple_of(owner * gb, gb), gb)

    own = [
        pltpu.make_async_copy(hidden, ah.at[h_block(col)], own_sem.at[0]),
        pltpu.make_async_copy(grad, ag.at[g_block(row)], own_sem.at[1]),
    ]
    for c in own:
        c.start()

    barrier = pltpu.get_barrier_semaphore()
    peers = [sibling, across] + [x_peer(d) for d in range(1, nx)] + [z_peer(d) for d in range(1, nz)]
    for peer in peers:
        pl.semaphore_signal(barrier, inc=1, device_id=peer, device_id_type=MESH)
    pl.semaphore_wait(barrier, len(peers))

    sends = []
    for k in range(pieces):
        cols = pl.ds(k * wide, wide)
        for d in range(1, nx):
            c = remote(
                hidden.at[:, cols], ah.at[h_block(col), cols], hx_send.at[k, d - 1], hx_recv.at[k, d - 1], x_peer(d)
            )
            c.start()
            sends.append(c)
    for d in range(1, nz):
        c = remote(grad, ag.at[g_block(row)], gz_send.at[d - 1], gz_recv.at[d - 1], z_peer(d))
        c.start()
        sends.append(c)
    c = remote(grad, ag.at[g_block(row)], gy_send.at[0], gy_recv.at[0], across)
    c.start()
    sends.append(c)
    for k in range(pieces):
        cols = pl.ds(k * wide, wide)
        c = remote(hidden.at[:, cols], ah.at[h_block(col), cols], hc_send.at[k, 0], hc_recv.at[k, 0], sibling)
        c.start()
        sends.append(c)

    for d in range(1, nz):
        source = lax.rem(z + nz - d, nz) * 2 + y
        part = ag.at[g_block(source)]
        remote(part, part, gz_send.at[d - 1], gz_recv.at[d - 1], across).wait_recv()
        c = remote(part, part, gy_send.at[d], gy_recv.at[d], across)
        c.start()
        sends.append(c)
    for k in range(pieces):
        cols = pl.ds(k * wide, wide)
        for d in range(1, nx):
            source = lax.rem(x + nx - d, nx) * 2 + core
            part = ah.at[h_block(source), cols]
            remote(part, part, hx_send.at[k, d - 1], hx_recv.at[k, d - 1], sibling).wait_recv()
            c = remote(part, part, hc_send.at[k, d], hc_recv.at[k, d], sibling)
            c.start()
            sends.append(c)
    for c in own:
        c.wait()
    for c in w_copies:
        c.wait()
    for k in range(pieces):
        cols = pl.ds(k * wide, wide)
        for d in range(nx):
            source = lax.rem(x + nx - d, nx) * 2 + 1 - core
            part = ah.at[h_block(source), cols]
            remote(part, part, hc_send.at[k, d], hc_recv.at[k, d], sibling).wait_recv()
    for d in range(nz):
        source = lax.rem(z + nz - d, nz) * 2 + 1 - y
        part = ag.at[g_block(source)]
        remote(part, part, gy_send.at[d], gy_recv.at[d], across).wait_recv()

    outs = [
        pltpu.make_async_copy(ah, all_hidden_out, out_sem.at[0]),
        pltpu.make_async_copy(ag, all_grad_out, out_sem.at[1]),
    ]
    for c in outs:
        c.start()

    def y_copy(t):
        return remote(p_part.at[t, 1 - y], p_recv.at[t], py_send.at[t], py_recv.at[t], across)

    def z_copy(t, d):
        return remote(
            p_part.at[t, y, lax.rem(z + d, nz)], p_recv_z.at[t, d - 1], pz_send.at[t, d - 1], pz_recv.at[t, d - 1], z_peer(d)
        )

    def c_copy(t):
        return remote(h_part.at[t, 1 - core], h_recv.at[t], qc_send.at[t], qc_recv.at[t], sibling)

    def x_copy(t, d):
        return remote(
            h_part.at[t, core, lax.rem(x + d, nx)], h_recv_x.at[t, d - 1], qx_send.at[t, d - 1], qx_recv.at[t, d - 1], x_peer(d)
        )

    def p_second(t):
        y_copy(t).wait_recv()
        p_part[t, y] += p_recv[t]
        for d in range(1, nz):
            z_copy(t, d).start()

    def h_second(t):
        c_copy(t).wait_recv()
        h_part[t, core] += h_recv[t]
        for d in range(1, nx):
            x_copy(t, d).start()

    @pl.loop(0, nh)
    def _(t):
        @pl.when(t < np_)
        def _():
            cols = pl.ds(pl.multiple_of(t * tp, tp), tp)
            value = jnp.dot(ah[...], w[:, cols], preferred_element_type=jnp.float32)
            for r in range(nrow):
                p_part[t, r % 2, r // 2] = value[r * gb : (r + 1) * gb]
            y_copy(t).start()

        rows = pl.ds(pl.multiple_of(t * th, th), th)
        value = lax.dot_general(ag[...], w[rows, :], (((1,), (1,)), ((), ())), preferred_element_type=jnp.float32)
        for c in range(ncol):
            h_part[t, c % 2, c // 2] = value[c * hb : (c + 1) * hb]
        c_copy(t).start()

        @pl.when(t >= 1)
        def _():
            h_second(t - 1)

    h_second(nh - 1)

    @pl.loop(0, np_)
    def _(t):
        p_second(t)

    @pl.loop(0, nh)
    def _(t):
        total = h_part[t, core, x]
        for d in range(1, nx):
            x_copy(t, d).wait_recv()
            total += h_recv_x[t, d - 1]
        hgrad_out[:, pl.ds(pl.multiple_of(t * th, th), th)] = total.astype(hgrad_out.dtype)

    @pl.loop(0, np_)
    def _(t):
        total = p_part[t, y, z]
        for d in range(1, nz):
            z_copy(t, d).wait_recv()
            total += p_recv_z[t, d - 1]
        proj_out[:, pl.ds(pl.multiple_of(t * tp, tp), tp)] = total.astype(proj_out.dtype)

    for c in sends:
        c.wait_send()
    for c in outs:
        c.wait()

    @pl.loop(0, np_)
    def _(t):
        y_copy(t).wait_send()
        for d in range(1, nz):
            z_copy(t, d).wait_send()

    @pl.loop(0, nh)
    def _(t):
        c_copy(t).wait_send()
        for d in range(1, nx):
            x_copy(t, d).wait_send()


def exchange(nrow, ncol, hidden, weight, grad):
    nz, nx = nrow // 2, ncol // 2
    hb, ff = hidden.shape
    gb, dd = grad.shape
    tp, th = tile_of(dd, 512), tile_of(ff, 512)
    np_, nh = dd // tp, ff // th
    np_ = min(np_, nh)
    tp = dd // np_
    pieces = 2 if ff % 256 == 0 else 1
    f32, bf16 = jnp.float32, jnp.bfloat16
    dma = pltpu.SemaphoreType.DMA
    any_spec = pl.BlockSpec(memory_space=pl.ANY)
    vmem_spec = pl.BlockSpec(memory_space=pltpu.VMEM)
    return pl.pallas_call(
        functools.partial(exchange_kernel, nrow, ncol),
        out_shape=(
            jax.ShapeDtypeStruct((gb, dd), bf16),
            jax.ShapeDtypeStruct((hb, ff), bf16),
            jax.ShapeDtypeStruct((hb * ncol, ff), bf16),
            jax.ShapeDtypeStruct((gb * nrow, dd), bf16),
        ),
        in_specs=[any_spec] * 3,
        out_specs=(vmem_spec, vmem_spec, any_spec, any_spec),
        scratch_shapes=[
            pltpu.VMEM((ff, dd), bf16),
            pltpu.VMEM((hb * ncol, ff), bf16),
            pltpu.VMEM((gb * nrow, dd), bf16),
            pltpu.VMEM((np_, 2, nz, gb, tp), f32),
            pltpu.VMEM((np_, nz, gb, tp), f32),
            pltpu.VMEM((np_, nz - 1, gb, tp), f32),
            pltpu.VMEM((nh, 2, nx, hb, th), f32),
            pltpu.VMEM((nh, nx, hb, th), f32),
            pltpu.VMEM((nh, nx - 1, hb, th), f32),
            dma((nh,)),
            dma((2,)),
            dma((2,)),
            dma((pieces, nx - 1)),
            dma((pieces, nx - 1)),
            dma((pieces, nx)),
            dma((pieces, nx)),
            dma((nz - 1,)),
            dma((nz - 1,)),
            dma((nz,)),
            dma((nz,)),
            dma((np_,)),
            dma((np_,)),
            dma((np_, nz - 1)),
            dma((np_, nz - 1)),
            dma((nh,)),
            dma((nh,)),
            dma((nh, nx - 1)),
            dma((nh, nx - 1)),
        ],
        compiler_params=pltpu.CompilerParams(
            collective_id=0, has_side_effects=True, vmem_limit_bytes=48 * 1024 * 1024
        ),
    )(hidden, weight, grad)


def outer_kernel(scale, h, g, out):
    value = lax.dot_general(h[...], g[...], (((0,), (0,)), ((), ())), preferred_element_type=jnp.float32)
    out[...] = value * scale


def outer(all_hidden, all_grad):
    tokens, ff = all_hidden.shape
    dd = all_grad.shape[1]
    th = tile_of(ff, 512)
    return pl.pallas_call(
        functools.partial(outer_kernel, tokens**-0.5),
        grid=(ff // th,),
        out_shape=jax.ShapeDtypeStruct((ff, dd), jnp.float32),
        in_specs=[pl.BlockSpec((tokens, th), lambda i: (0, i)), pl.BlockSpec((tokens, dd), lambda i: (0, 0))],
        out_specs=pl.BlockSpec((th, dd), lambda i: (i, 0)),
        compiler_params=pltpu.CompilerParams(vmem_limit_bytes=40 * 1024 * 1024),
        cost_estimate=pl.CostEstimate(
            flops=2 * tokens * ff * dd, bytes_accessed=4 * ff * dd + 2 * tokens * (ff + dd), transcendentals=0
        ),
    )(all_hidden, all_grad)


def solution(mesh):
    nrow, ncol = mesh.shape["row"], mesh.shape["col"]

    def on_device(hidden, down_weight, out_grad):
        projected, hidden_grad, all_hidden, all_grad = exchange(nrow, ncol, hidden, down_weight, out_grad)
        return projected, hidden_grad, outer(all_hidden, all_grad)

    return jax.shard_map(
        on_device,
        mesh=mesh,
        in_specs=(P("col", "row"), P("row", "col"), P("row", "col")),
        out_specs=(P("row", "col"), P("col", "row"), P("row", "col")),
        check_vma=False,
    )
```

time: 132 us -> 54.7 us (0.41)
  Pallas kernels: 0 us -> 50.7 us
  blocking collectives: 43.2 us -> 0 us
  waiting for transfers between devices: 38.7 us -> 0 us
  matrix products: 32 us -> 0 us
  between operations: 14.1 us -> 0.65 us
  other arithmetic: 3.27 us -> 0 us
  local copies, waits for them, and re-layouts: 0.01 us -> 3.09 us
    pallas_call x0 -> x2, Pallas kernels: none -> 50.7 us  [the longest x1 39.7 us: exchange(): pl.pallas_call(functools.partial(exchange_kernel, nrow, ncol), out_shape=...]
    all_gather x2 -> x0, blocking collectives: 43.2 us -> none  [the longest x1 32.2 us: on_device(): all_grad = lax.all_gather(out_grad, 'row', axis=0, tiled=True)]
    reduce_scatter x2 -> x0, waiting for transfers between devices: 38.6 us -> none  [the longest x1 30 us: on_device(): lax.psum_scatter(partial_grad, 'col', scatter_dimension=0, tiled=True)]
    dot_general x3 -> x0, matrix products: 32 us -> none  [the longest x1 12.4 us: on_device(): lax.dot_general(all_hidden, all_grad, (((0,), (0,)), ((), ())), preferred...]
    convert_element_type x2 -> x0, other arithmetic: 3.27 us -> none  [the longest x1 1.73 us: on_device(): lax.psum_scatter(partial_grad, 'col', scatter_dimension=0, tiled=True)]
    unnamed x2 -> x6, local copies, waits for them, and re-layouts: 0.01 us -> 3.09 us
  transfers between devices with their start and end apart: 2 -> 0, of which waited for: 2 -> 0; matrix products, arithmetic and copies ran while one was open for 19% -> 0% of each run, Pallas kernels for 0% -> 0%
where the time goes in v1:
time: 54.7 us; the launch traced here: 54.5 us
  Pallas kernels  50.7 us (93%)
  local copies, waits for them, and re-layouts  3.09 us (6%)
  between operations  0.65 us (1%)
    pallas_call x1, Pallas kernels, exchange(): pl.pallas_call(functools.partial(exchange_kernel, nrow, ncol), out_shape=...  39.7 us
    pallas_call x1, Pallas kernels, outer(): pl.pallas_call(functools.partial(outer_kernel, tokens ** (-0.5)), grid=(f...  11 us
    unnamed x6, local copies, waits for them, and re-layouts  3.09 us

profile of v1, /device:TPU:0, one launch (start us, length us, event | category | flops | bytes accessed | tf_op | source)
XLA Modules:
  0.0 54.5 jit_solution(571240834086597269)
XLA Ops:
  0.6 0.0 copy-start
  0.6 0.9 %copy-done = bf16[32,3584]{1,0:T(8,128)(2,1)S(1)} copy-done((bf16[32,3584]{1,0:T(8,128)(2,1)S(1)}, bf16[32,3584]{1,0:T(8,128)(2,1)}, u32[]{:S(2)}) %copy-start) | copy-done | bytes 229400
  1.6 0.0 copy-start.1
  1.6 0.8 %copy-done.1 = bf16[16,2048]{1,0:T(8,128)(2,1)S(1)} copy-done((bf16[16,2048]{1,0:T(8,128)(2,1)S(1)}, bf16[16,2048]{1,0:T(8,128)(2,1)}, u32[]{:S(2)}) %copy-start.1) | copy-done | bytes 65560
  2.4 39.7 %shard_map.58 = (bf16[16,2048]{1,0:T(8,128)(2,1)S(1)}, bf16[32,3584]{1,0:T(8,128)(2,1)S(1)}, bf16[128,3584]{1,0:T(8,128)(2,1)S(1)}, bf16[128,2048]{1,0:T(8,128)(2,1)S(1)}) custom-call(bf16[32,3584]{1,0:T(8,128)(2,1)S(1)} %copy-done, bf16[3584,2048]{1,0:T(8,128)(2,1)} %weight.1, bf16[16,2048]{1,0:T(8,128)(2,1)S(1)} %copy-done.1), custom_call_target="tpu_custom_call" | custom-call | tf_op jit(solution)/shard_map/pallas_call | solution.py:272
  42.1 11.0 %shard_map.59 = f32[3584,2048]{1,0:T(8,128)} custom-call(bf16[128,3584]{1,0:T(8,128)(2,1)S(1)} %get-tuple-element.9.h, bf16[128,2048]{1,0:T(8,128)(2,1)S(1)} %get-tuple-element.10.g), custom_call_target="tpu_custom_call" | custom-call | flops 1879048192 | bytes 30801920 | tf_op jit(solution)/shard_map/pallas_call | solution.py:327
  53.2 0.6 %copy.8 = bf16[16,2048]{1,0:T(8,128)(2,1)} copy(bf16[16,2048]{1,0:T(8,128)(2,1)S(1)} %get-tuple-element.14) | data formatting | bytes 131072
  53.8 0.7 %copy.9 = bf16[32,3584]{1,0:T(8,128)(2,1)} copy(bf16[32,3584]{1,0:T(8,128)(2,1)S(1)} %get-tuple-element.15) | data formatting | bytes 458752
Async XLA Ops:
  0.6 0.9 %copy-start = (bf16[32,3584]{1,0:T(8,128)(2,1)S(1)}, bf16[32,3584]{1,0:T(8,128)(2,1)}, u32[]{:S(2)}) copy-start(bf16[32,3584]{1,0:T(8,128)(2,1)} %hidden.1) | copy-start | bytes 688132
  1.6 0.8 %copy-start.1 = (bf16[16,2048]{1,0:T(8,128)(2,1)S(1)}, bf16[16,2048]{1,0:T(8,128)(2,1)}, u32[]{:S(2)}) copy-start(bf16[16,2048]{1,0:T(8,128)(2,1)} %grad.1) | copy-start | bytes 196612

commit v2 on v1

--- a/solution.py
+++ b/solution.py
@@ -24,8 +24,21 @@
     hidden,
     weight,
     grad,
-    proj_out,
-    hgrad_out,
+    *refs,
+):
+    nz, nx = nrow // 2, ncol // 2
+    p_out, h_out, rest = refs[:nz], refs[nz : nz + nx], refs[nz + nx :]
+    exchange_body(nrow, ncol, p_out, h_out, hidden, weight, grad, *rest)
+
+
+def exchange_body(
+    nrow,
+    ncol,
+    p_out,
+    h_out,
+    hidden,
+    weight,
+    grad,
     all_hidden_out,
     all_grad_out,
     w,
@@ -33,10 +46,8 @@
     ag,
     p_part,
     p_recv,
-    p_recv_z,
     h_part,
     h_recv,
-    h_recv_x,
     w_sem,
     own_sem,
     out_sem,
@@ -50,12 +61,8 @@
     gy_recv,
     py_send,
     py_recv,
-    pz_send,
-    pz_recv,
     qc_send,
     qc_recv,
-    qx_send,
-    qx_recv,
 ):
     nz, nx = nrow // 2, ncol // 2
     row, col = lax.axis_index("row"), lax.axis_index("col")
@@ -130,22 +137,28 @@
         c.start()
         sends.append(c)
 
-    for d in range(1, nz):
+    def forward_grad(d):
         source = lax.rem(z + nz - d, nz) * 2 + y
         part = ag.at[g_block(source)]
         remote(part, part, gz_send.at[d - 1], gz_recv.at[d - 1], across).wait_recv()
         c = remote(part, part, gy_send.at[d], gy_recv.at[d], across)
         c.start()
         sends.append(c)
-    for k in range(pieces):
-        cols = pl.ds(k * wide, wide)
-        for d in range(1, nx):
-            source = lax.rem(x + nx - d, nx) * 2 + core
-            part = ah.at[h_block(source), cols]
-            remote(part, part, hx_send.at[k, d - 1], hx_recv.at[k, d - 1], sibling).wait_recv()
-            c = remote(part, part, hc_send.at[k, d], hc_recv.at[k, d], sibling)
-            c.start()
-            sends.append(c)
+
+    def forward_hidden(k, d):
+        source = lax.rem(x + nx - d, nx) * 2 + core
+        part = ah.at[h_block(source), pl.ds(k * wide, wide)]
+        remote(part, part, hx_send.at[k, d - 1], hx_recv.at[k, d - 1], sibling).wait_recv()
+        c = remote(part, part, hc_send.at[k, d], hc_recv.at[k, d], sibling)
+        c.start()
+        sends.append(c)
+
+    from_x = [(k, d) for k in range(pieces) for d in range(1, nx)]
+    for step in range(max(nz - 1, len(from_x))):
+        if step < nz - 1:
+            forward_grad(step + 1)
+        if step < len(from_x):
+            forward_hidden(*from_x[step])
     for c in own:
         c.wait()
     for c in w_copies:
@@ -156,11 +169,39 @@
             source = lax.rem(x + nx - d, nx) * 2 + 1 - core
             part = ah.at[h_block(source), cols]
             remote(part, part, hc_send.at[k, d], hc_recv.at[k, d], sibling).wait_recv()
+
+    def y_copy(t):
+        return remote(p_part.at[t, 1 - y], p_recv.at[t], py_send.at[t], py_recv.at[t], across)
+
+    def c_copy(t):
+        return remote(h_part.at[t, 1 - core], h_recv.at[t], qc_send.at[t], qc_recv.at[t], sibling)
+
+    def p_second(t):
+        y_copy(t).wait_recv()
+        cols = pl.ds(pl.multiple_of(t * tp, tp), tp)
+        for d in range(nz):
+            at = lax.rem(z + d, nz)
+            p_out[d][:, cols] = p_part[t, y, at] + p_recv[t, at]
+
+    def h_second(t):
+        c_copy(t).wait_recv()
+        cols = pl.ds(pl.multiple_of(t * th, th), th)
+        for d in range(nx):
+            at = lax.rem(x + d, nx)
+            h_out[d][:, cols] = h_part[t, core, at] + h_recv[t, at]
+
+    @pl.loop(0, np_)
+    def _(t):
+        cols = pl.ds(pl.multiple_of(t * tp, tp), tp)
+        value = jnp.dot(ah[...], w[:, cols], preferred_element_type=jnp.float32)
+        for r in range(nrow):
+            p_part[t, r % 2, r // 2] = value[r * gb : (r + 1) * gb]
+        y_copy(t).start()
+
     for d in range(nz):
         source = lax.rem(z + nz - d, nz) * 2 + 1 - y
         part = ag.at[g_block(source)]
         remote(part, part, gy_send.at[d], gy_recv.at[d], across).wait_recv()
-
     outs = [
         pltpu.make_async_copy(ah, all_hidden_out, out_sem.at[0]),
         pltpu.make_async_copy(ag, all_grad_out, out_sem.at[1]),
@@ -168,44 +209,8 @@
     for c in outs:
         c.start()
 
-    def y_copy(t):
-        return remote(p_part.at[t, 1 - y], p_recv.at[t], py_send.at[t], py_recv.at[t], across)
-
-    def z_copy(t, d):
-        return remote(
-            p_part.at[t, y, lax.rem(z + d, nz)], p_recv_z.at[t, d - 1], pz_send.at[t, d - 1], pz_recv.at[t, d - 1], z_peer(d)
-        )
-
-    def c_copy(t):
-        return remote(h_part.at[t, 1 - core], h_recv.at[t], qc_send.at[t], qc_recv.at[t], sibling)
-
-    def x_copy(t, d):
-        return remote(
-            h_part.at[t, core, lax.rem(x + d, nx)], h_recv_x.at[t, d - 1], qx_send.at[t, d - 1], qx_recv.at[t, d - 1], x_peer(d)
-        )
-
-    def p_second(t):
-        y_copy(t).wait_recv()
-        p_part[t, y] += p_recv[t]
-        for d in range(1, nz):
-            z_copy(t, d).start()
-
-    def h_second(t):
-        c_copy(t).wait_recv()
-        h_part[t, core] += h_recv[t]
-        for d in range(1, nx):
-            x_copy(t, d).start()
-
     @pl.loop(0, nh)
     def _(t):
-        @pl.when(t < np_)
-        def _():
-            cols = pl.ds(pl.multiple_of(t * tp, tp), tp)
-            value = jnp.dot(ah[...], w[:, cols], preferred_element_type=jnp.float32)
-            for r in range(nrow):
-                p_part[t, r % 2, r // 2] = value[r * gb : (r + 1) * gb]
-            y_copy(t).start()
-
         rows = pl.ds(pl.multiple_of(t * th, th), th)
         value = lax.dot_general(ag[...], w[rows, :], (((1,), (1,)), ((), ())), preferred_element_type=jnp.float32)
         for c in range(ncol):
@@ -222,22 +227,6 @@
     def _(t):
         p_second(t)
 
-    @pl.loop(0, nh)
-    def _(t):
-        total = h_part[t, core, x]
-        for d in range(1, nx):
-            x_copy(t, d).wait_recv()
-            total += h_recv_x[t, d - 1]
-        hgrad_out[:, pl.ds(pl.multiple_of(t * th, th), th)] = total.astype(hgrad_out.dtype)
-
-    @pl.loop(0, np_)
-    def _(t):
-        total = p_part[t, y, z]
-        for d in range(1, nz):
-            z_copy(t, d).wait_recv()
-            total += p_recv_z[t, d - 1]
-        proj_out[:, pl.ds(pl.multiple_of(t * tp, tp), tp)] = total.astype(proj_out.dtype)
-
     for c in sends:
         c.wait_send()
     for c in outs:
@@ -246,14 +235,10 @@
     @pl.loop(0, np_)
     def _(t):
         y_copy(t).wait_send()
-        for d in range(1, nz):
-            z_copy(t, d).wait_send()
 
     @pl.loop(0, nh)
     def _(t):
         c_copy(t).wait_send()
-        for d in range(1, nx):
-            x_copy(t, d).wait_send()
 
 
 def exchange(nrow, ncol, hidden, weight, grad):
@@ -272,23 +257,21 @@
     return pl.pallas_call(
         functools.partial(exchange_kernel, nrow, ncol),
         out_shape=(
-            jax.ShapeDtypeStruct((gb, dd), bf16),
-            jax.ShapeDtypeStruct((hb, ff), bf16),
+            *[jax.ShapeDtypeStruct((gb, dd), f32)] * nz,
+            *[jax.ShapeDtypeStruct((hb, ff), f32)] * nx,
             jax.ShapeDtypeStruct((hb * ncol, ff), bf16),
             jax.ShapeDtypeStruct((gb * nrow, dd), bf16),
         ),
         in_specs=[any_spec] * 3,
-        out_specs=(vmem_spec, vmem_spec, any_spec, any_spec),
+        out_specs=(*[vmem_spec] * (nz + nx), any_spec, any_spec),
         scratch_shapes=[
             pltpu.VMEM((ff, dd), bf16),
             pltpu.VMEM((hb * ncol, ff), bf16),
             pltpu.VMEM((gb * nrow, dd), bf16),
             pltpu.VMEM((np_, 2, nz, gb, tp), f32),
             pltpu.VMEM((np_, nz, gb, tp), f32),
-            pltpu.VMEM((np_, nz - 1, gb, tp), f32),
             pltpu.VMEM((nh, 2, nx, hb, th), f32),
             pltpu.VMEM((nh, nx, hb, th), f32),
-            pltpu.VMEM((nh, nx - 1, hb, th), f32),
             dma((nh,)),
             dma((2,)),
             dma((2,)),
@@ -302,12 +285,8 @@
             dma((nz,)),
             dma((np_,)),
             dma((np_,)),
-            dma((np_, nz - 1)),
-            dma((np_, nz - 1)),
             dma((nh,)),
             dma((nh,)),
-            dma((nh, nx - 1)),
-            dma((nh, nx - 1)),
         ],
         compiler_params=pltpu.CompilerParams(
             collective_id=0, has_side_effects=True, vmem_limit_bytes=48 * 1024 * 1024
@@ -340,9 +319,23 @@
 def solution(mesh):
     nrow, ncol = mesh.shape["row"], mesh.shape["col"]
 
+    nz, nx = nrow // 2, ncol // 2
+
+    def shifted(value, axis, groups, d):
+        pairs = [(g * 2 + o, (g + d) % groups * 2 + o) for g in range(groups) for o in range(2)]
+        return lax.ppermute(value, axis, pairs)
+
     def on_device(hidden, down_weight, out_grad):
-        projected, hidden_grad, all_hidden, all_grad = exchange(nrow, ncol, hidden, down_weight, out_grad)
-        return projected, hidden_grad, outer(all_hidden, all_grad)
+        *sums, all_hidden, all_grad = exchange(nrow, ncol, hidden, down_weight, out_grad)
+        p_sums, h_sums = sums[:nz], sums[nz:]
+        h_total = h_sums[0]
+        for d in range(1, nx):
+            h_total += shifted(h_sums[d], "col", nx, d)
+        p_total = p_sums[0]
+        for d in range(1, nz):
+            p_total += shifted(p_sums[d], "row", nz, d)
+        weight_grad = outer(all_hidden, all_grad)
+        return p_total.astype(jnp.bfloat16), h_total.astype(jnp.bfloat16), weight_grad
 
     return jax.shard_map(
         on_device,

time: 54.7 us -> 48.1 us (0.88)
  Pallas kernels: 50.7 us -> 38.3 us
  starting transfers between devices: 0 us -> 5.83 us
  other arithmetic: 0 us -> 1.39 us
  local copies, waits for them, and re-layouts: 3.09 us -> 1.77 us
    pallas_call x1, Pallas kernels: 39.7 us -> 27.2 us  [exchange(): pl.pallas_call(functools.partial(exchange_kernel, nrow, ncol), out_shape=...]
    ppermute x0 -> x4, starting transfers between devices: none -> 5.83 us  [shifted(): return lax.ppermute(value, axis, pairs)]
    convert_element_type x0 -> x2, other arithmetic: none -> 1.39 us  [the longest x1 0.73 us: on_device(): h_total.astype(jnp.bfloat16)]
    unnamed x6 -> x4, local copies, waits for them, and re-layouts: 3.09 us -> 1.77 us
  transfers between devices with their start and end apart: 0 -> 4, of which waited for: 0 -> 0; matrix products, arithmetic and copies ran while one was open for 0% -> 1% of each run, Pallas kernels for 0% -> 23%
where the time goes in v2:
time: 48.1 us; the launch traced here: 47.9 us
  Pallas kernels  38.3 us (80%)
  starting transfers between devices  5.83 us (12%)
  local copies, waits for them, and re-layouts  1.77 us (4%)
  other arithmetic  1.39 us (3%)
  between operations  0.66 us (1%)
    pallas_call x1, Pallas kernels, exchange(): pl.pallas_call(functools.partial(exchange_kernel, nrow, ncol), out_shape=...  27.2 us
    pallas_call x1, Pallas kernels, outer(): pl.pallas_call(functools.partial(outer_kernel, tokens ** (-0.5)), grid=(f...  11 us
    ppermute x4, starting transfers between devices, shifted(): return lax.ppermute(value, axis, pairs)  5.83 us
    unnamed x4, local copies, waits for them, and re-layouts  1.77 us
  transfers between devices with their start and end apart: 4, of which 0 were waited for; matrix products, arithmetic and copies ran while one was open for 1% of the time, Pallas kernels for 23%

profile of v2, /device:TPU:0, one launch (start us, length us, event | category | flops | bytes accessed | tf_op | source)
XLA Modules:
  0.0 47.9 jit_solution(4145953003601880886)
XLA Ops:
  0.6 0.0 copy-start
  0.6 0.9 %copy-done = bf16[32,3584]{1,0:T(8,128)(2,1)S(1)} copy-done((bf16[32,3584]{1,0:T(8,128)(2,1)S(1)}, bf16[32,3584]{1,0:T(8,128)(2,1)}, u32[]{:S(2)}) %copy-start) | copy-done | bytes 229400
  1.6 0.0 copy-start.1
  1.6 0.8 %copy-done.1 = bf16[16,2048]{1,0:T(8,128)(2,1)S(1)} copy-done((bf16[16,2048]{1,0:T(8,128)(2,1)S(1)}, bf16[16,2048]{1,0:T(8,128)(2,1)}, u32[]{:S(2)}) %copy-start.1) | copy-done | bytes 65560
  2.4 27.2 %shard_map.58 = (f32[16,2048]{1,0:T(8,128)S(1)}, f32[16,2048]{1,0:T(8,128)S(1)}, f32[16,2048]{1,0:T(8,128)S(1)}, f32[16,2048]{1,0:T(8,128)S(1)}, f32[32,3584]{1,...) custom-call(bf16[32,3584]{1,0:T(8,128)(2,1)S(1)} %copy-done, ...), custom_call_target="tpu_custom_call" | custom-call | tf_op jit(solution)/shard_map/pallas_call | solution.py:257
  29.7 0.6 %collective-permute-start = (f32[16,2048]{1,0:T(8,128)S(1)}, f32[16,2048]{1,0:T(8,128)S(1)}, u32[]{:S(2)}, u32[]{:S(2)}) collective-permute-start(f32[16,2048]{1,0:T(8,128)S(1)} %get-tuple-element.12), channel_id=1, source_target_pairs={{0,8},{4,12},{8,16},{12,20},{16,24},{20,28},{24,0},{28,4},{1,9},{5... | collective-permute-start | bytes 393224 | tf_op jit(solution)/shard_map/ppermute | solution.py:326
  30.3 3.5 %collective-permute-start.1 = (f32[16,2048]{1,0:T(8,128)S(1)}, f32[16,2048]{1,0:T(8,128)S(1)}, u32[]{:S(2)}, u32[]{:S(2)}) collective-permute-start(f32[16,2048]{1,0:T(8,128)S(1)} %get-tuple-element.13), channel_id=1, source_target_pairs={{0,16},{4,20},{8,24},{12,28},{16,0},{20,4},{24,8},{28,12},{1,17},{... | collective-permute-start | bytes 393224 | tf_op jit(solution)/shard_map/ppermute | solution.py:326
  33.7 0.0 collective-permute-start.2
  33.7 1.7 %collective-permute-start.3 = (f32[32,3584]{1,0:T(8,128)S(1)}, f32[32,3584]{1,0:T(8,128)S(1)}, u32[]{:S(2)}, u32[]{:S(2)}) collective-permute-start(f32[32,3584]{1,0:T(8,128)S(1)} %get-tuple-element.16), channel_id=1, source_target_pairs={{0,2},{1,3},{2,0},{3,1},{4,6},{5,7},{6,4},{7,5},{8,10},{9,11},{10,... | collective-permute-start | bytes 1376264 | tf_op jit(solution)/shard_map/ppermute | solution.py:326
  35.5 11.0 %shard_map.59 = f32[3584,2048]{1,0:T(8,128)} custom-call(bf16[128,3584]{1,0:T(8,128)(2,1)S(1)} %get-tuple-element.17.h, bf16[128,2048]{1,0:T(8,128)(2,1)S(1)} %get-tuple-element.18.g), custom_call_target="tpu_custom_call" | custom-call | flops 1879048192 | bytes 30801920 | tf_op jit(solution)/shard_map/pallas_call | solution.py:306
  46.5 0.0 collective-permute-done
  46.5 0.0 collective-permute-done.1
  46.5 0.0 collective-permute-done.2
  46.5 0.7 %add_convert_fusion.1 = bf16[16,2048]{1,0:T(8,128)(2,1)} fusion(f32[16,2048]{1,0:T(8,128)S(1)} %collective-permute-done.2, f32[16,2048]{1,0:T(8,128)S(1)} %collective-permute-done.1, f32[16,2048]{1,0:T(8,128)S(1)} %get-tuple-element.11, f32[16,2048]{1,0:T(8,128)S(1)} %collective-permute-done), kind=kLoop, calls=%fused_computation.1 | loop fusion | flops 131072 | bytes 589824 | tf_op jit(solution)/shard_map/convert_element_type | solution.py:338
  47.2 0.0 collective-permute-done.3
  47.2 0.7 %add_convert_fusion = bf16[32,3584]{1,0:T(8,128)(2,1)} fusion(f32[32,3584]{1,0:T(8,128)S(1)} %get-tuple-element.15, f32[32,3584]{1,0:T(8,128)S(1)} %collective-permute-done.3), kind=kLoop, calls=%fused_computation | loop fusion | flops 229376 | bytes 1146880 | tf_op jit(solution)/shard_map/convert_element_type | solution.py:338
Async XLA Ops:
  0.6 0.9 %copy-start = (bf16[32,3584]{1,0:T(8,128)(2,1)S(1)}, bf16[32,3584]{1,0:T(8,128)(2,1)}, u32[]{:S(2)}) copy-start(bf16[32,3584]{1,0:T(8,128)(2,1)} %hidden.1) | copy-start | bytes 688132
  1.6 0.8 %copy-start.1 = (bf16[16,2048]{1,0:T(8,128)(2,1)S(1)}, bf16[16,2048]{1,0:T(8,128)(2,1)}, u32[]{:S(2)}) copy-start(bf16[16,2048]{1,0:T(8,128)(2,1)} %grad.1) | copy-start | bytes 196612
  29.7 16.8 %collective-permute-start = (f32[16,2048]{1,0:T(8,128)S(1)}, f32[16,2048]{1,0:T(8,128)S(1)}, u32[]{:S(2)}, u32[]{:S(2)}) collective-permute-start(f32[16,2048]{1,0:T(8,128)S(1)} %get-tuple-element.12), channel_id=1, source_target_pairs={{0,8},{4,12},{8,16},{12,20},{16,24},{20,28},{24,0},{28,4},{1,9},{5... | collective-permute-start | bytes 393224 | tf_op jit(solution)/shard_map/ppermute | solution.py:326
  30.3 16.2 %collective-permute-start.1 = (f32[16,2048]{1,0:T(8,128)S(1)}, f32[16,2048]{1,0:T(8,128)S(1)}, u32[]{:S(2)}, u32[]{:S(2)}) collective-permute-start(f32[16,2048]{1,0:T(8,128)S(1)} %get-tuple-element.13), channel_id=1, source_target_pairs={{0,16},{4,20},{8,24},{12,28},{16,0},{20,4},{24,8},{28,12},{1,17},{... | collective-permute-start | bytes 393224 | tf_op jit(solution)/shard_map/ppermute | solution.py:326
  33.7 12.8 %collective-permute-start.2 = (f32[16,2048]{1,0:T(8,128)S(1)}, f32[16,2048]{1,0:T(8,128)S(1)}, u32[]{:S(2)}, u32[]{:S(2)}) collective-permute-start(f32[16,2048]{1,0:T(8,128)S(1)} %get-tuple-element.14), channel_id=1, source_target_pairs={{0,24},{4,28},{8,0},{12,4},{16,8},{20,12},{24,16},{28,20},{1,25},{... | collective-permute-start | bytes 393224 | tf_op jit(solution)/shard_map/ppermute | solution.py:326
  33.7 13.4 %collective-permute-start.3 = (f32[32,3584]{1,0:T(8,128)S(1)}, f32[32,3584]{1,0:T(8,128)S(1)}, u32[]{:S(2)}, u32[]{:S(2)}) collective-permute-start(f32[32,3584]{1,0:T(8,128)S(1)} %get-tuple-element.16), channel_id=1, source_target_pairs={{0,2},{1,3},{2,0},{3,1},{4,6},{5,7},{6,4},{7,5},{8,10},{9,11},{10,... | collective-permute-start | bytes 1376264 | tf_op jit(solution)/shard_map/ppermute | solution.py:326

commit v3 on v2

--- a/solution.py
+++ b/solution.py
@@ -21,19 +21,22 @@
 def exchange_kernel(
     nrow,
     ncol,
+    early,
     hidden,
     weight,
     grad,
     *refs,
 ):
     nz, nx = nrow // 2, ncol // 2
-    p_out, h_out, rest = refs[:nz], refs[nz : nz + nx], refs[nz + nx :]
-    exchange_body(nrow, ncol, p_out, h_out, hidden, weight, grad, *rest)
+    outputs = nz + early
+    p_out, h_out, rest = refs[:outputs], refs[outputs : outputs + nx], refs[outputs + nx :]
+    exchange_body(nrow, ncol, early, p_out, h_out, hidden, weight, grad, *rest)
 
 
 def exchange_body(
     nrow,
     ncol,
+    nf,
     p_out,
     h_out,
     hidden,
@@ -46,6 +49,8 @@
     ag,
     p_part,
     p_recv,
+    z_recv,
+    y_last,
     h_part,
     h_recv,
     w_sem,
@@ -61,6 +66,10 @@
     gy_recv,
     py_send,
     py_recv,
+    pz_send,
+    pz_recv,
+    pl_send,
+    pl_recv,
     qc_send,
     qc_recv,
 ):
@@ -163,22 +172,40 @@
         c.wait()
     for c in w_copies:
         c.wait()
-    for k in range(pieces):
-        cols = pl.ds(k * wide, wide)
+
+    def arrived(k):
         for d in range(nx):
             source = lax.rem(x + nx - d, nx) * 2 + 1 - core
-            part = ah.at[h_block(source), cols]
+            part = ah.at[h_block(source), pl.ds(k * wide, wide)]
             remote(part, part, hc_send.at[k, d], hc_recv.at[k, d], sibling).wait_recv()
 
     def y_copy(t):
         return remote(p_part.at[t, 1 - y], p_recv.at[t], py_send.at[t], py_recv.at[t], across)
 
+    def z_copy(d):
+        return remote(
+            p_part.at[0, :, lax.rem(z + d, nz)], z_recv.at[d - 1], pz_send.at[d - 1], pz_recv.at[d - 1], z_peer(d)
+        )
+
+    def last_copy():
+        return remote(p_part.at[0, 1 - y, z], y_last, pl_send.at[0], pl_recv.at[0], across)
+
+    def z_sum():
+        for d in range(1, nz):
+            z_copy(d).wait_recv()
+        for half in range(2):
+            total = p_part[0, half, z]
+            for d in range(1, nz):
+                total += z_recv[d - 1, half]
+            p_part[0, half, z] = total
+        last_copy().start()
+
     def c_copy(t):
         return remote(h_part.at[t, 1 - core], h_recv.at[t], qc_send.at[t], qc_recv.at[t], sibling)
 
     def p_second(t):
         y_copy(t).wait_recv()
-        cols = pl.ds(pl.multiple_of(t * tp, tp), tp)
+        cols = pl.ds(pl.multiple_of((t - nf) * tp, tp), tp)
         for d in range(nz):
             at = lax.rem(z + d, nz)
             p_out[d][:, cols] = p_part[t, y, at] + p_recv[t, at]
@@ -190,13 +217,24 @@
             at = lax.rem(x + d, nx)
             h_out[d][:, cols] = h_part[t, core, at] + h_recv[t, at]
 
+    for k in range(pieces):
+        arrived(k)
+
     @pl.loop(0, np_)
     def _(t):
         cols = pl.ds(pl.multiple_of(t * tp, tp), tp)
         value = jnp.dot(ah[...], w[:, cols], preferred_element_type=jnp.float32)
         for r in range(nrow):
             p_part[t, r % 2, r // 2] = value[r * gb : (r + 1) * gb]
-        y_copy(t).start()
+
+        @pl.when(t >= nf)
+        def _():
+            y_copy(t).start()
+
+        @pl.when(t < nf)
+        def _():
+            for d in range(1, nz):
+                z_copy(d).start()
 
     for d in range(nz):
         source = lax.rem(z + nz - d, nz) * 2 + 1 - y
@@ -221,18 +259,27 @@
         def _():
             h_second(t - 1)
 
+    if nf:
+        z_sum()
     h_second(nh - 1)
 
-    @pl.loop(0, np_)
+    @pl.loop(nf, np_)
     def _(t):
         p_second(t)
+
+    if nf:
+        last_copy().wait_recv()
+        p_out[nz][...] = p_part[0, y, z] + y_last[...]
+        last_copy().wait_send()
+        for d in range(1, nz):
+            z_copy(d).wait_send()
 
     for c in sends:
         c.wait_send()
     for c in outs:
         c.wait()
 
-    @pl.loop(0, np_)
+    @pl.loop(nf, np_)
     def _(t):
         y_copy(t).wait_send()
 
@@ -249,27 +296,32 @@
     np_, nh = dd // tp, ff // th
     np_ = min(np_, nh)
     tp = dd // np_
+    early = 1 if np_ > 2 else 0
+    kept = [jax.ShapeDtypeStruct((gb, tp), jnp.float32)] * early
     pieces = 2 if ff % 256 == 0 else 1
     f32, bf16 = jnp.float32, jnp.bfloat16
     dma = pltpu.SemaphoreType.DMA
     any_spec = pl.BlockSpec(memory_space=pl.ANY)
     vmem_spec = pl.BlockSpec(memory_space=pltpu.VMEM)
     return pl.pallas_call(
-        functools.partial(exchange_kernel, nrow, ncol),
+        functools.partial(exchange_kernel, nrow, ncol, early),
         out_shape=(
-            *[jax.ShapeDtypeStruct((gb, dd), f32)] * nz,
+            *[jax.ShapeDtypeStruct((gb, dd - early * tp), f32)] * nz,
+            *kept,
             *[jax.ShapeDtypeStruct((hb, ff), f32)] * nx,
             jax.ShapeDtypeStruct((hb * ncol, ff), bf16),
             jax.ShapeDtypeStruct((gb * nrow, dd), bf16),
         ),
         in_specs=[any_spec] * 3,
-        out_specs=(*[vmem_spec] * (nz + nx), any_spec, any_spec),
+        out_specs=(*[vmem_spec] * (nz + early + nx), any_spec, any_spec),
         scratch_shapes=[
             pltpu.VMEM((ff, dd), bf16),
             pltpu.VMEM((hb * ncol, ff), bf16),
             pltpu.VMEM((gb * nrow, dd), bf16),
             pltpu.VMEM((np_, 2, nz, gb, tp), f32),
             pltpu.VMEM((np_, nz, gb, tp), f32),
+            pltpu.VMEM((nz - 1, 2, gb, tp), f32),
+            pltpu.VMEM((gb, tp), f32),
             pltpu.VMEM((nh, 2, nx, hb, th), f32),
             pltpu.VMEM((nh, nx, hb, th), f32),
             dma((nh,)),
@@ -285,6 +337,10 @@
             dma((nz,)),
             dma((np_,)),
             dma((np_,)),
+            dma((nz - 1,)),
+            dma((nz - 1,)),
+            dma((1,)),
+            dma((1,)),
             dma((nh,)),
             dma((nh,)),
         ],
@@ -327,13 +383,14 @@
 
     def on_device(hidden, down_weight, out_grad):
         *sums, all_hidden, all_grad = exchange(nrow, ncol, hidden, down_weight, out_grad)
-        p_sums, h_sums = sums[:nz], sums[nz:]
+        p_sums, early, h_sums = sums[:nz], sums[nz:-nx], sums[-nx:]
         h_total = h_sums[0]
         for d in range(1, nx):
             h_total += shifted(h_sums[d], "col", nx, d)
         p_total = p_sums[0]
         for d in range(1, nz):
             p_total += shifted(p_sums[d], "row", nz, d)
+        p_total = jnp.concatenate([*early, p_total], axis=1)
         weight_grad = outer(all_hidden, all_grad)
         return p_total.astype(jnp.bfloat16), h_total.astype(jnp.bfloat16), weight_grad
 

time: 48.1 us -> 46.6 us (0.969)
  starting transfers between devices: 5.83 us -> 4.51 us
    ppermute x4, starting transfers between devices: 5.83 us -> 4.51 us  [shifted(): return lax.ppermute(value, axis, pairs)]
    convert_element_type x1 -> x0, other arithmetic: 0.66 us -> none  [on_device(): p_total.astype(jnp.bfloat16)]
    concatenate x0 -> x1, other arithmetic: none -> 0.64 us  [on_device(): p_total = jnp.concatenate([*early, p_total], axis=1)]
  transfers between devices with their start and end apart: 4 -> 4, of which waited for: 0 -> 0; matrix products, arithmetic and copies ran while one was open for 1% -> 1% of each run, Pallas kernels for 23% -> 24%
where the time goes in v3:
time: 46.6 us; the launch traced here: 46.4 us
  Pallas kernels  38.1 us (82%)
  starting transfers between devices  4.51 us (10%)
  local copies, waits for them, and re-layouts  1.77 us (4%)
  other arithmetic  1.4 us (3%)
  between operations  0.66 us (1%)
    pallas_call x1, Pallas kernels, exchange(): pl.pallas_call(functools.partial(exchange_kernel, nrow, ncol, early), out...  27.1 us
    pallas_call x1, Pallas kernels, outer(): pl.pallas_call(functools.partial(outer_kernel, tokens ** (-0.5)), grid=(f...  11 us
    ppermute x4, starting transfers between devices, shifted(): return lax.ppermute(value, axis, pairs)  4.51 us
    unnamed x4, local copies, waits for them, and re-layouts  1.77 us
  transfers between devices with their start and end apart: 4, of which 0 were waited for; matrix products, arithmetic and copies ran while one was open for 1% of the time, Pallas kernels for 24%

profile of v3, /device:TPU:0, one launch (start us, length us, event | category | flops | bytes accessed | tf_op | source)
XLA Modules:
  0.0 46.4 jit_solution(708532949174828235)
XLA Ops:
  0.6 0.0 copy-start
  0.6 0.9 %copy-done = bf16[32,3584]{1,0:T(8,128)(2,1)S(1)} copy-done((bf16[32,3584]{1,0:T(8,128)(2,1)S(1)}, bf16[32,3584]{1,0:T(8,128)(2,1)}, u32[]{:S(2)}) %copy-start) | copy-done | bytes 229400
  1.6 0.0 copy-start.1
  1.6 0.8 %copy-done.1 = bf16[16,2048]{1,0:T(8,128)(2,1)S(1)} copy-done((bf16[16,2048]{1,0:T(8,128)(2,1)S(1)}, bf16[16,2048]{1,0:T(8,128)(2,1)}, u32[]{:S(2)}) %copy-start.1) | copy-done | bytes 65560
  2.4 27.1 %shard_map.58 = (f32[16,1536]{1,0:T(8,128)S(1)}, f32[16,1536]{1,0:T(8,128)S(1)}, f32[16,1536]{1,0:T(8,128)S(1)}, f32[16,1536]{1,0:T(8,128)S(1)}, f32[16,512]{1,0...) custom-call(bf16[32,3584]{1,0:T(8,128)(2,1)S(1)} %copy-done, ...), custom_call_target="tpu_custom_call" | custom-call | tf_op jit(solution)/shard_map/pallas_call | solution.py:306
  29.5 0.6 %collective-permute-start = (f32[16,1536]{1,0:T(8,128)S(1)}, f32[16,1536]{1,0:T(8,128)S(1)}, u32[]{:S(2)}, u32[]{:S(2)}) collective-permute-start(f32[16,1536]{1,0:T(8,128)S(1)} %get-tuple-element.14), channel_id=1, source_target_pairs={{0,8},{4,12},{8,16},{12,20},{16,24},{20,28},{24,0},{28,4},{1,9},{5... | collective-permute-start | bytes 294920 | tf_op jit(solution)/shard_map/ppermute | solution.py:382
  30.1 2.1 %collective-permute-start.1 = (f32[16,1536]{1,0:T(8,128)S(1)}, f32[16,1536]{1,0:T(8,128)S(1)}, u32[]{:S(2)}, u32[]{:S(2)}) collective-permute-start(f32[16,1536]{1,0:T(8,128)S(1)} %get-tuple-element.15), channel_id=1, source_target_pairs={{0,16},{4,20},{8,24},{12,28},{16,0},{20,4},{24,8},{28,12},{1,17},{... | collective-permute-start | bytes 294920 | tf_op jit(solution)/shard_map/ppermute | solution.py:382
  32.3 1.1 %collective-permute-start.2 = (f32[16,1536]{1,0:T(8,128)S(1)}, f32[16,1536]{1,0:T(8,128)S(1)}, u32[]{:S(2)}, u32[]{:S(2)}) collective-permute-start(f32[16,1536]{1,0:T(8,128)S(1)} %get-tuple-element.16), channel_id=1, source_target_pairs={{0,24},{4,28},{8,0},{12,4},{16,8},{20,12},{24,16},{28,20},{1,25},{... | collective-permute-start | bytes 294920 | tf_op jit(solution)/shard_map/ppermute | solution.py:382
  33.4 0.6 %collective-permute-start.3 = (f32[32,3584]{1,0:T(8,128)S(1)}, f32[32,3584]{1,0:T(8,128)S(1)}, u32[]{:S(2)}, u32[]{:S(2)}) collective-permute-start(f32[32,3584]{1,0:T(8,128)S(1)} %get-tuple-element.18), channel_id=1, source_target_pairs={{0,2},{1,3},{2,0},{3,1},{4,6},{5,7},{6,4},{7,5},{8,10},{9,11},{10,... | collective-permute-start | bytes 1376264 | tf_op jit(solution)/shard_map/ppermute | solution.py:382
  34.0 11.0 %shard_map.59 = f32[3584,2048]{1,0:T(8,128)} custom-call(bf16[128,3584]{1,0:T(8,128)(2,1)S(1)} %get-tuple-element.19.h, bf16[128,2048]{1,0:T(8,128)(2,1)S(1)} %get-tuple-element.20.g), custom_call_target="tpu_custom_call" | custom-call | flops 1879048192 | bytes 30801920 | tf_op jit(solution)/shard_map/pallas_call | solution.py:362
  45.0 0.0 collective-permute-done
  45.0 0.0 collective-permute-done.1
  45.0 0.0 collective-permute-done.2
  45.1 0.6 %pad_maximum_fusion = bf16[16,2048]{1,0:T(8,128)(2,1)} fusion(bf16[16,1536]{1,0:T(8,128)(2,1)S(1)} %add_convert_fusion.1, bf16[16,512]{1,0:T(8,128)(2,1)S(1)} %convert.6), kind=kLoop, calls=%fused_computation.2 | loop fusion | flops 131072 | bytes 131072 | tf_op jit(solution)/shard_map/concatenate | solution.py:393
  45.7 0.0 collective-permute-done.3
  45.7 0.7 %add_convert_fusion = bf16[32,3584]{1,0:T(8,128)(2,1)} fusion(f32[32,3584]{1,0:T(8,128)S(1)} %get-tuple-element.17, f32[32,3584]{1,0:T(8,128)S(1)} %collective-permute-done.3), kind=kLoop, calls=%fused_computation | loop fusion | flops 229376 | bytes 1146880 | tf_op jit(solution)/shard_map/convert_element_type | solution.py:395
  (2 shorter events, 0.0 us)
Async XLA Ops:
  0.6 0.9 %copy-start = (bf16[32,3584]{1,0:T(8,128)(2,1)S(1)}, bf16[32,3584]{1,0:T(8,128)(2,1)}, u32[]{:S(2)}) copy-start(bf16[32,3584]{1,0:T(8,128)(2,1)} %hidden.1) | copy-start | bytes 688132
  1.6 0.8 %copy-start.1 = (bf16[16,2048]{1,0:T(8,128)(2,1)S(1)}, bf16[16,2048]{1,0:T(8,128)(2,1)}, u32[]{:S(2)}) copy-start(bf16[16,2048]{1,0:T(8,128)(2,1)} %grad.1) | copy-start | bytes 196612
  29.5 15.5 %collective-permute-start = (f32[16,1536]{1,0:T(8,128)S(1)}, f32[16,1536]{1,0:T(8,128)S(1)}, u32[]{:S(2)}, u32[]{:S(2)}) collective-permute-start(f32[16,1536]{1,0:T(8,128)S(1)} %get-tuple-element.14), channel_id=1, source_target_pairs={{0,8},{4,12},{8,16},{12,20},{16,24},{20,28},{24,0},{28,4},{1,9},{5... | collective-permute-start | bytes 294920 | tf_op jit(solution)/shard_map/ppermute | solution.py:382
  30.1 14.9 %collective-permute-start.1 = (f32[16,1536]{1,0:T(8,128)S(1)}, f32[16,1536]{1,0:T(8,128)S(1)}, u32[]{:S(2)}, u32[]{:S(2)}) collective-permute-start(f32[16,1536]{1,0:T(8,128)S(1)} %get-tuple-element.15), channel_id=1, source_target_pairs={{0,16},{4,20},{8,24},{12,28},{16,0},{20,4},{24,8},{28,12},{1,17},{... | collective-permute-start | bytes 294920 | tf_op jit(solution)/shard_map/ppermute | solution.py:382
  32.3 12.8 %collective-permute-start.2 = (f32[16,1536]{1,0:T(8,128)S(1)}, f32[16,1536]{1,0:T(8,128)S(1)}, u32[]{:S(2)}, u32[]{:S(2)}) collective-permute-start(f32[16,1536]{1,0:T(8,128)S(1)} %get-tuple-element.16), channel_id=1, source_target_pairs={{0,24},{4,28},{8,0},{12,4},{16,8},{20,12},{24,16},{28,20},{1,25},{... | collective-permute-start | bytes 294920 | tf_op jit(solution)/shard_map/ppermute | solution.py:382
  33.4 12.3 %collective-permute-start.3 = (f32[32,3584]{1,0:T(8,128)S(1)}, f32[32,3584]{1,0:T(8,128)S(1)}, u32[]{:S(2)}, u32[]{:S(2)}) collective-permute-start(f32[32,3584]{1,0:T(8,128)S(1)} %get-tuple-element.18), channel_id=1, source_target_pairs={{0,2},{1,3},{2,0},{3,1},{4,6},{5,7},{6,4},{7,5},{8,10},{9,11},{10,... | collective-permute-start | bytes 1376264 | tf_op jit(solution)/shard_map/ppermute | solution.py:382

commit v4 on v3

--- a/solution.py
+++ b/solution.py
@@ -312,7 +312,7 @@
             jax.ShapeDtypeStruct((hb * ncol, ff), bf16),
             jax.ShapeDtypeStruct((gb * nrow, dd), bf16),
         ),
-        in_specs=[any_spec] * 3,
+        in_specs=[vmem_spec, any_spec, vmem_spec],
         out_specs=(*[vmem_spec] * (nz + early + nx), any_spec, any_spec),
         scratch_shapes=[
             pltpu.VMEM((ff, dd), bf16),

time: 46.6 us -> 46.6 us (level)
  no operation moved by 1% of the time
where the time goes in v4:
time: 46.6 us; the launch traced here: 46.4 us
  Pallas kernels  38.1 us (82%)
  starting transfers between devices  4.51 us (10%)
  local copies, waits for them, and re-layouts  1.77 us (4%)
  other arithmetic  1.4 us (3%)
  between operations  0.66 us (1%)
    pallas_call x1, Pallas kernels, exchange(): pl.pallas_call(functools.partial(exchange_kernel, nrow, ncol, early), out...  27.1 us
    pallas_call x1, Pallas kernels, outer(): pl.pallas_call(functools.partial(outer_kernel, tokens ** (-0.5)), grid=(f...  11 us
    ppermute x4, starting transfers between devices, shifted(): return lax.ppermute(value, axis, pairs)  4.51 us
    unnamed x4, local copies, waits for them, and re-layouts  1.77 us
  transfers between devices with their start and end apart: 4, of which 0 were waited for; matrix products, arithmetic and copies ran while one was open for 1% of the time, Pallas kernels for 24%

profile of v4, /device:TPU:0, one launch (start us, length us, event | category | flops | bytes accessed | tf_op | source)
XLA Modules:
  0.0 46.4 jit_solution(708532949174828235)
XLA Ops:
  0.6 0.0 copy-start
  0.6 0.9 %copy-done = bf16[32,3584]{1,0:T(8,128)(2,1)S(1)} copy-done((bf16[32,3584]{1,0:T(8,128)(2,1)S(1)}, bf16[32,3584]{1,0:T(8,128)(2,1)}, u32[]{:S(2)}) %copy-start) | copy-done | bytes 229400
  1.6 0.0 copy-start.1
  1.6 0.8 %copy-done.1 = bf16[16,2048]{1,0:T(8,128)(2,1)S(1)} copy-done((bf16[16,2048]{1,0:T(8,128)(2,1)S(1)}, bf16[16,2048]{1,0:T(8,128)(2,1)}, u32[]{:S(2)}) %copy-start.1) | copy-done | bytes 65560
  2.4 27.1 %shard_map.58 = (f32[16,1536]{1,0:T(8,128)S(1)}, f32[16,1536]{1,0:T(8,128)S(1)}, f32[16,1536]{1,0:T(8,128)S(1)}, f32[16,1536]{1,0:T(8,128)S(1)}, f32[16,512]{1,0...) custom-call(bf16[32,3584]{1,0:T(8,128)(2,1)S(1)} %copy-done, ...), custom_call_target="tpu_custom_call" | custom-call | tf_op jit(solution)/shard_map/pallas_call | solution.py:306
  29.5 0.6 %collective-permute-start = (f32[16,1536]{1,0:T(8,128)S(1)}, f32[16,1536]{1,0:T(8,128)S(1)}, u32[]{:S(2)}, u32[]{:S(2)}) collective-permute-start(f32[16,1536]{1,0:T(8,128)S(1)} %get-tuple-element.14), channel_id=1, source_target_pairs={{0,8},{4,12},{8,16},{12,20},{16,24},{20,28},{24,0},{28,4},{1,9},{5... | collective-permute-start | bytes 294920 | tf_op jit(solution)/shard_map/ppermute | solution.py:382
  30.1 2.1 %collective-permute-start.1 = (f32[16,1536]{1,0:T(8,128)S(1)}, f32[16,1536]{1,0:T(8,128)S(1)}, u32[]{:S(2)}, u32[]{:S(2)}) collective-permute-start(f32[16,1536]{1,0:T(8,128)S(1)} %get-tuple-element.15), channel_id=1, source_target_pairs={{0,16},{4,20},{8,24},{12,28},{16,0},{20,4},{24,8},{28,12},{1,17},{... | collective-permute-start | bytes 294920 | tf_op jit(solution)/shard_map/ppermute | solution.py:382
  32.3 1.1 %collective-permute-start.2 = (f32[16,1536]{1,0:T(8,128)S(1)}, f32[16,1536]{1,0:T(8,128)S(1)}, u32[]{:S(2)}, u32[]{:S(2)}) collective-permute-start(f32[16,1536]{1,0:T(8,128)S(1)} %get-tuple-element.16), channel_id=1, source_target_pairs={{0,24},{4,28},{8,0},{12,4},{16,8},{20,12},{24,16},{28,20},{1,25},{... | collective-permute-start | bytes 294920 | tf_op jit(solution)/shard_map/ppermute | solution.py:382
  33.4 0.6 %collective-permute-start.3 = (f32[32,3584]{1,0:T(8,128)S(1)}, f32[32,3584]{1,0:T(8,128)S(1)}, u32[]{:S(2)}, u32[]{:S(2)}) collective-permute-start(f32[32,3584]{1,0:T(8,128)S(1)} %get-tuple-element.18), channel_id=1, source_target_pairs={{0,2},{1,3},{2,0},{3,1},{4,6},{5,7},{6,4},{7,5},{8,10},{9,11},{10,... | collective-permute-start | bytes 1376264 | tf_op jit(solution)/shard_map/ppermute | solution.py:382
  34.0 11.0 %shard_map.59 = f32[3584,2048]{1,0:T(8,128)} custom-call(bf16[128,3584]{1,0:T(8,128)(2,1)S(1)} %get-tuple-element.19.h, bf16[128,2048]{1,0:T(8,128)(2,1)S(1)} %get-tuple-element.20.g), custom_call_target="tpu_custom_call" | custom-call | flops 1879048192 | bytes 30801920 | tf_op jit(solution)/shard_map/pallas_call | solution.py:362
  45.0 0.0 collective-permute-done
  45.0 0.0 collective-permute-done.1
  45.0 0.0 collective-permute-done.2
  45.1 0.6 %pad_maximum_fusion = bf16[16,2048]{1,0:T(8,128)(2,1)} fusion(bf16[16,1536]{1,0:T(8,128)(2,1)S(1)} %add_convert_fusion.1, bf16[16,512]{1,0:T(8,128)(2,1)S(1)} %convert.6), kind=kLoop, calls=%fused_computation.2 | loop fusion | flops 131072 | bytes 131072 | tf_op jit(solution)/shard_map/concatenate | solution.py:393
  45.7 0.0 collective-permute-done.3
  45.7 0.7 %add_convert_fusion = bf16[32,3584]{1,0:T(8,128)(2,1)} fusion(f32[32,3584]{1,0:T(8,128)S(1)} %get-tuple-element.17, f32[32,3584]{1,0:T(8,128)S(1)} %collective-permute-done.3), kind=kLoop, calls=%fused_computation | loop fusion | flops 229376 | bytes 1146880 | tf_op jit(solution)/shard_map/convert_element_type | solution.py:395
  (2 shorter events, 0.0 us)
Async XLA Ops:
  0.6 0.9 %copy-start = (bf16[32,3584]{1,0:T(8,128)(2,1)S(1)}, bf16[32,3584]{1,0:T(8,128)(2,1)}, u32[]{:S(2)}) copy-start(bf16[32,3584]{1,0:T(8,128)(2,1)} %hidden.1) | copy-start | bytes 688132
  1.6 0.8 %copy-start.1 = (bf16[16,2048]{1,0:T(8,128)(2,1)S(1)}, bf16[16,2048]{1,0:T(8,128)(2,1)}, u32[]{:S(2)}) copy-start(bf16[16,2048]{1,0:T(8,128)(2,1)} %grad.1) | copy-start | bytes 196612
  29.5 15.5 %collective-permute-start = (f32[16,1536]{1,0:T(8,128)S(1)}, f32[16,1536]{1,0:T(8,128)S(1)}, u32[]{:S(2)}, u32[]{:S(2)}) collective-permute-start(f32[16,1536]{1,0:T(8,128)S(1)} %get-tuple-element.14), channel_id=1, source_target_pairs={{0,8},{4,12},{8,16},{12,20},{16,24},{20,28},{24,0},{28,4},{1,9},{5... | collective-permute-start | bytes 294920 | tf_op jit(solution)/shard_map/ppermute | solution.py:382
  30.1 14.9 %collective-permute-start.1 = (f32[16,1536]{1,0:T(8,128)S(1)}, f32[16,1536]{1,0:T(8,128)S(1)}, u32[]{:S(2)}, u32[]{:S(2)}) collective-permute-start(f32[16,1536]{1,0:T(8,128)S(1)} %get-tuple-element.15), channel_id=1, source_target_pairs={{0,16},{4,20},{8,24},{12,28},{16,0},{20,4},{24,8},{28,12},{1,17},{... | collective-permute-start | bytes 294920 | tf_op jit(solution)/shard_map/ppermute | solution.py:382
  32.3 12.8 %collective-permute-start.2 = (f32[16,1536]{1,0:T(8,128)S(1)}, f32[16,1536]{1,0:T(8,128)S(1)}, u32[]{:S(2)}, u32[]{:S(2)}) collective-permute-start(f32[16,1536]{1,0:T(8,128)S(1)} %get-tuple-element.16), channel_id=1, source_target_pairs={{0,24},{4,28},{8,0},{12,4},{16,8},{20,12},{24,16},{28,20},{1,25},{... | collective-permute-start | bytes 294920 | tf_op jit(solution)/shard_map/ppermute | solution.py:382
  33.4 12.3 %collective-permute-start.3 = (f32[32,3584]{1,0:T(8,128)S(1)}, f32[32,3584]{1,0:T(8,128)S(1)}, u32[]{:S(2)}, u32[]{:S(2)}) collective-permute-start(f32[32,3584]{1,0:T(8,128)S(1)} %get-tuple-element.18), channel_id=1, source_target_pairs={{0,2},{1,3},{2,0},{3,1},{4,6},{5,7},{6,4},{7,5},{8,10},{9,11},{10,... | collective-permute-start | bytes 1376264 | tf_op jit(solution)/shard_map/ppermute | solution.py:382
